TPU v7x, 32 devices: a whole 2x2x4 slice. The times are simulated.
32 devices in a mesh: dp: 4 (over y, x), tensor: 8 (over z, core).
Axes of the slice: x: 2, y: 2, z: 4, core: 2. Of those that a mesh axis runs over, the one named last changes fastest.
Arguments:
- tokens: bfloat16 [1024, 3072], P('dp', 'tensor'), may hold values from -6 to 6
- buckets: int32 [1024], P('dp'), may hold values from 0 to 999
- modulation: float32 [1000, 3, 3072], P(None, None, 'tensor'), may hold values from -3 to 3
- up_weight: bfloat16 [3072, 12288], P(None, 'tensor'), may hold values from -0.109375 to 0.109375
- down_weight: bfloat16 [3072, 12288], P(None, 'tensor'), may hold values from -0.0546875 to 0.0546875
- output_cotangent: bfloat16 [1024, 3072], P('dp', 'tensor'), may hold values from -6 to 6
Outputs:
- mixed: bfloat16 [1024, 3072], P('dp', 'tensor')
- token_input_gradient: bfloat16 [1024, 3072], P('dp', 'tensor')
- grad_up: float32 [3072, 12288], P('dp', 'tensor')
- grad_down: float32 [3072, 12288], P('dp', 'tensor')
All inputs are finite; a program needn't handle non-finite values.
Results may differ from a plain program's by a relative error of at most 0.0062.
Values may be sent and summed in bfloat16 or wider, within the bound.
No kernel may reach another device: no remote copies, remote signals or barrier semaphores. Data moves between devices by JAX's collectives and lax.ppermute only.
A program may use at most 128 MiB of HBM per device.

v0:
```python
import jax
import jax.numpy as jnp
from jax import lax
from jax.sharding import PartitionSpec as P


def gelu_tanh(value):
    return jax.nn.gelu(value, approximate=True)


def on_device(tokens, buckets, modulation, up_weight, down_weight, output_cotangent):
    local_cols = tokens.shape[1]
    model_width = local_cols * lax.axis_size("tensor")
    input_tokens = tokens.astype(jnp.float32)
    cond = jnp.take(modulation, buckets, axis=0)
    modulation_shift = cond[:, 0]
    modulation_scale = cond[:, 1]
    gate = cond[:, 2]
    total, squares = lax.psum(
        (jnp.sum(input_tokens, axis=1), jnp.sum(input_tokens * input_tokens, axis=1)), "tensor"
    )
    row_mean = total / model_width
    var = squares / model_width - row_mean * row_mean
    inverse_deviation = lax.rsqrt(var + 1e-06)
    normalized_input = (input_tokens - row_mean[:, None]) * inverse_deviation[:, None]
    hidden_input_rows = (normalized_input * (1.0 + modulation_scale) + modulation_shift).astype(
        jnp.bfloat16
    )
    full_in = lax.all_gather(hidden_input_rows, "tensor", axis=1, tiled=True)
    pre = jnp.dot(full_in, up_weight, preferred_element_type=jnp.float32)
    act = gelu_tanh(pre).astype(jnp.bfloat16)
    block = down_weight
    velocity = lax.psum_scatter(
        lax.dot_general(block, act, (((1,), (1,)), ((), ())), preferred_element_type=jnp.float32),
        "tensor",
        scatter_dimension=0,
        tiled=True,
    ).T
    mixed = (input_tokens + gate * velocity).astype(jnp.bfloat16)
    dvel = (output_cotangent.astype(jnp.float32) * gate).astype(jnp.bfloat16)
    full_dvel = lax.all_gather(dvel, "tensor", axis=1, tiled=True)
    dact = jnp.dot(full_dvel, down_weight, preferred_element_type=jnp.float32)
    pull = jax.vjp(gelu_tanh, pre)[1]
    dpre = pull(dact)[0].astype(jnp.bfloat16)
    block = up_weight
    dh = lax.psum_scatter(
        lax.dot_general(block, dpre, (((1,), (1,)), ((), ())), preferred_element_type=jnp.float32),
        "tensor",
        scatter_dimension=0,
        tiled=True,
    ).T
    normalized_input_gradient = dh * (1.0 + modulation_scale)
    first_product, second_product = lax.psum(
        (
            jnp.sum(normalized_input_gradient, axis=1),
            jnp.sum(normalized_input_gradient * normalized_input, axis=1),
        ),
        "tensor",
    )
    token_input_gradient = output_cotangent.astype(jnp.float32) + inverse_deviation[:, None] * (
        normalized_input_gradient
        - first_product[:, None] / model_width
        - normalized_input * second_product[:, None] / model_width
    )
    cols = full_in
    grad_up = lax.psum_scatter(
        lax.dot_general(cols, dpre, (((0,), (0,)), ((), ())), preferred_element_type=jnp.float32),
        "dp",
        scatter_dimension=0,
        tiled=True,
    )
    cols = full_dvel
    grad_down = lax.psum_scatter(
        lax.dot_general(cols, act, (((0,), (0,)), ((), ())), preferred_element_type=jnp.float32),
        "dp",
        scatter_dimension=0,
        tiled=True,
    )
    return (mixed, token_input_gradient.astype(jnp.bfloat16), grad_up, grad_down)


def solution(mesh):
    placed = (
        P("dp", "tensor"),
        P("dp"),
        P(None, None, "tensor"),
        P(None, "tensor"),
        P(None, "tensor"),
        P("dp", "tensor"),
    )
    return jax.shard_map(
        on_device,
        mesh=mesh,
        in_specs=placed,
        out_specs=(P("dp", "tensor"), P("dp", "tensor"), P("dp", "tensor"), P("dp", "tensor")),
        check_vma=False,
    )
```

profile of v0, /device:TPU:0, one launch (start us, length us, event | category | flops | bytes accessed | tf_op | source)
XLA Modules:
  0.0 537.5 jit_solution(13374361323119234266)
XLA Ops:
  8.6 1.1 convert_reduce_fusion
  9.7 18.1 %all-reduce.1 = (f32[256]{0:T(256)S(1)}, f32[256]{0:T(256)S(1)}) all-reduce(f32[256]{0:T(256)S(1)} %get-tuple-element.7, f32[256]{0:T(256)S(1)} %get-tuple-element.6), channel_id=1, replica_groups=mesh['dp'=4,'tensor'=8] {'tensor'}, use_global_device_ids=true, to_apply=%region_3.4 | all-reduce | flops 512 | bytes 4096 | tf_op jit(solution)/shard_map/psum | solution.py:19
  27.8 4.1 gather_fusion
  32.0 0.7 copy-done
  32.9 0.9 fusion.7
  33.9 0.7 all-gather.3.cloned.1.call-update
  34.6 22.8 %all-gather.5.cloned.1.call-done = bf16[256,3072]{1,0:T(8,128)(2,1)} async-done(((bf16[256,384]{1,0:T(8,128)(2,1)}), bf16[256,3072]{1,0:T(8,128)(2,1)}) %all-gather.5.cloned.1.call-update) | async-done | bytes 1572880 | tf_op jit(solution)/shard_map/all_gather | solution.py:41
  57.4 7.9 %fusion.24 = f32[256,1536]{1,0:T(8,128)} fusion(bf16[256,3072]{1,0:T(8,128)(2,1)} %all-gather.5.cloned.1.call-done, bf16[3072,1536]{1,0:T(8,128)(2,1)} %param.10), kind=kOutput, calls=%fused_computation.48 | convolution fusion | flops 2415919104 | bytes 12582912 | tf_op jit(solution)/shard_map/dot_general | solution.py:42
  65.3 18.7 %all-gather.3.cloned.1.call-done = bf16[256,3072]{1,0:T(8,128)(2,1)} async-done(((bf16[256,384]{1,0:T(8,128)(2,1)}), bf16[256,3072]{1,0:T(8,128)(2,1)}) %all-gather.3.cloned.1.call-update) | async-done | bytes 1572880 | tf_op jit(solution)/shard_map/all_gather | solution.py:29
  84.0 7.9 %fusion.6 = (bf16[256,1536]{1,0:T(8,128)(2,1)S(1)}, f32[256,1536]{1,0:T(8,128)S(1)}) fusion(f32[256,1536]{1,0:T(8,128)} %fusion.24, bf16[256,3072]{1,0:T(8,128)(2,1)} %all-gather.3.cloned.1.call-done, bf16[3072,1536]{1,0:T(8,128)(2,1)} %param.9), kind=kOutput, calls=%fused_computation.11 | convolution fusion | flops 2423783424 | bytes 14942208 | tf_op jit(solution)/shard_map/dot_general | solution.py:30
  92.0 0.9 copy-done.4
  92.9 8.0 %convolution_bitcast_fusion = f32[3072,256]{0,1:T(8,128)} fusion(bf16[256,1536]{1,0:T(8,128)(2,1)S(1)} %get-tuple-element.18, bf16[3072,1536]{1,0:T(8,128)(2,1)} %param.9), kind=kOutput, calls=%fused_computation.1 | convolution fusion | flops 2415919104 | bytes 13369344 | tf_op jit(solution)/shard_map/dot_general | solution.py:47
  101.0 8.1 %convolution_bitcast_fusion.1 = f32[3072,256]{0,1:T(8,128)} fusion(bf16[3072,1536]{1,0:T(8,128)(2,1)} %param.10, f32[256,1536]{1,0:T(8,128)S(1)} %get-tuple-element.19), kind=kOutput, calls=%fused_computation.2 | convolution fusion | flops 2419458048 | bytes 14155776 | tf_op jit(solution)/shard_map/dot_general | solution.py:34
  109.3 1.2 copy-done.2
  110.4 9.6 %fusion.23 = f32[3072,1536]{1,0:T(8,128)} fusion(bf16[256,3072]{1,0:T(8,128)(2,1)S(1)} %copy-done.2, f32[256,1536]{1,0:T(8,128)} %copy-done.3), kind=kOutput, calls=%fused_computation.47 | convolution fusion | flops 2419458048 | bytes 22020096 | tf_op jit(solution)/shard_map/dot_general | solution.py:74
  120.1 1.4 copy-done.1
  121.4 9.2 %fusion.25 = f32[3072,1536]{1,0:T(8,128)} fusion(bf16[256,3072]{1,0:T(8,128)(2,1)S(1)} %copy-done.1, bf16[256,1536]{1,0:T(8,128)(2,1)} %copy-done.4), kind=kOutput, calls=%fused_computation.49 | convolution fusion | flops 2415919104 | bytes 21233664 | tf_op jit(solution)/shard_map/dot_general | solution.py:67
  130.7 9.9 %reduce-scatter.7.cloned.1.call-done = f32[384,256]{0,1:T(8,128)} async-done(((f32[3072,256]{0,1:T(8,128)}), f32[384,256]{0,1:T(8,128)}) %reduce-scatter.7.cloned.1.call-update) | async-done | bytes 393232 | tf_op jit(solution)/shard_map/reduce_scatter | solution.py:46
  140.6 1.2 fusion.22
  141.8 15.4 %all-reduce = (f32[256]{0:T(256)S(1)}, f32[256]{0:T(256)S(1)}) all-reduce(f32[256]{0:T(256)S(1)} %get-tuple-element.5, f32[256]{0:T(256)S(1)} %get-tuple-element.4), channel_id=1, replica_groups=mesh['dp'=4,'tensor'=8] {'tensor'}, use_global_device_ids=true, to_apply=%region_9.10 | all-reduce | flops 512 | bytes 4096 | tf_op jit(solution)/shard_map/psum | solution.py:53
  157.2 25.1 %reduce-scatter.5.cloned.1.call-done = f32[384,256]{0,1:T(8,128)} async-done(((f32[3072,256]{0,1:T(8,128)}), f32[384,256]{0,1:T(8,128)}) %reduce-scatter.5.cloned.1.call-update) | async-done | bytes 393232 | tf_op jit(solution)/shard_map/reduce_scatter | solution.py:33
  182.3 2.1 fusion.8
  184.4 171.6 %reduce-scatter.11.cloned.1.call-done = f32[768,1536]{1,0:T(8,128)} async-done(((f32[3072,1536]{1,0:T(8,128)}), f32[768,1536]{1,0:T(8,128)}) %reduce-scatter.11.cloned.1.call-update) | async-done | bytes 4718608 | tf_op jit(solution)/shard_map/reduce_scatter | solution.py:73
  355.9 174.7 %reduce-scatter.9.cloned.1.call-done = f32[768,1536]{1,0:T(8,128)} async-done(((f32[3072,1536]{1,0:T(8,128)}), f32[768,1536]{1,0:T(8,128)}) %reduce-scatter.9.cloned.1.call-update) | async-done | bytes 4718608 | tf_op jit(solution)/shard_map/reduce_scatter | solution.py:66
  (25 shorter events, 2.2 us)
Async XLA Ops:
  7.2 50.3 %all-gather.5.cloned.1.call-start = ((), (), s32[]{:S(2)}) async-start(), calls=%async_computation.6 | async-start | bytes 1769472 | tf_op jit(solution)/shard_map/all_gather | solution.py:41
  31.9 0.9 copy-start
  31.9 1.0 copy-start.5
  33.8 50.2 %all-gather.3.cloned.1.call-start = ((), (), s32[]{:S(2)}) async-start(), calls=%async_computation.4 | async-start | bytes 1769472 | tf_op jit(solution)/shard_map/all_gather | solution.py:29
  34.6 106.0 %reduce-scatter.7.cloned.1.call-start = ((), (), s32[]{:S(2)}) async-start(), calls=%async_computation.7 | async-start | bytes 3538944 | tf_op jit(solution)/shard_map/reduce_scatter | solution.py:46
  92.0 0.9 copy-start.4
  92.0 8.9 %copy-start.3 = (f32[256,1536]{1,0:T(8,128)}, f32[256,1536]{1,0:T(8,128)S(1)}, u32[]{:S(2)}) copy-start(f32[256,1536]{1,0:T(8,128)S(1)} %get-tuple-element.19) | copy-start | bytes 4718596
  100.9 81.4 %reduce-scatter.5.cloned.1.call-start = ((), (), s32[]{:S(2)}) async-start(), calls=%async_computation.5 | async-start | bytes 3538944 | tf_op jit(solution)/shard_map/reduce_scatter | solution.py:33
  109.0 1.4 copy-start.2
  109.0 246.9 %reduce-scatter.11.cloned.1.call-start = ((), (), s32[]{:S(2)}) async-start(), calls=%async_computation.9 | async-start | bytes 23592960 | tf_op jit(solution)/shard_map/reduce_scatter | solution.py:73
  120.0 1.4 copy-start.1
  120.0 410.6 %reduce-scatter.9.cloned.1.call-start = ((), (), s32[]{:S(2)}) async-start(), calls=%async_computation.8 | async-start | bytes 23592960 | tf_op jit(solution)/shard_map/reduce_scatter | solution.py:66
Sparse Core Ops, SparseCore 0:
  33.9 23.4 all-gather.4
  59.6 24.3 all-gather.2
  101.0 39.5 reduce-scatter.6
  142.7 39.5 reduce-scatter.4
  185.8 170.0 reduce-scatter.10
  359.8 170.8 reduce-scatter.8
where the time goes:
time: 538 us; the launch traced here: 537 us
  waiting for transfers between devices  424 us (79%)
  matrix products  50.7 us (9%)
  blocking collectives  33.4 us (6%)
  between operations  14.2 us (3%)
  local copies, waits for them, and re-layouts  8.32 us (2%)
  other arithmetic  6.84 us (1%)
    reduce_scatter x1, waiting for transfers between devices, on_device(): lax.psum_scatter(lax.dot_general(cols, dpre, (((0,), (0,)), ((), ())), pr...  175 us
    reduce_scatter x1, waiting for transfers between devices, on_device(): lax.psum_scatter(lax.dot_general(cols, act, (((0,), (0,)), ((), ())), pre...  172 us
    reduce_scatter x1, waiting for transfers between devices, on_device(): lax.psum_scatter(lax.dot_general(block, act, (((1,), (1,)), ((), ())), pr...  25.1 us
    all_gather x1, waiting for transfers between devices, on_device(): full_dvel = lax.all_gather(dvel, 'tensor', axis=1, tiled=True)  22.8 us
    all_gather x1, waiting for transfers between devices, on_device(): full_in = lax.all_gather(hidden_input_rows, 'tensor', axis=1, tiled=True)  18.7 us
    psum x1, blocking collectives, on_device(): lax.psum((jnp.sum(input_tokens, axis=1), jnp.sum(input_tokens * input_tok...  18.1 us
    psum x1, blocking collectives, on_device(): lax.psum((jnp.sum(normalized_input_gradient, axis=1), jnp.sum(normalized_...  15.4 us
  transfers between devices with their start and end apart: 6, of which 6 were waited for; matrix products, arithmetic and copies ran while one was open for 7% of the time, Pallas kernels for 0%

commit v1 on v0

v1 whole, which is shorter than its diff:
```python
import functools
import math

import jax
import jax.numpy as jnp
from jax import lax
from jax.experimental import pallas as pl
from jax.experimental.pallas import tpu as pltpu
from jax.sharding import PartitionSpec as P

GELU_C = math.sqrt(2.0 / math.pi)
GELU_A = 0.044715
MIB = 1024 * 1024
F32 = jnp.float32
BF16 = jnp.bfloat16


def gelu_and_slope(v):
    square = v * v
    t = jnp.tanh(GELU_C * v * (1.0 + GELU_A * square))
    half = 0.5 * (1.0 + t)
    slope = half + (0.5 * GELU_C) * v * (1.0 - t * t) * (1.0 + (3.0 * GELU_A) * square)
    return v * half, slope


def column_tiles(length):
    tile = next((t for t in (256, 128) if length % t == 0), length)
    return [slice(start, start + tile) for start in range(0, length, tile)]


def call(kernel, name, operands, outs, scratch, flops):
    return pl.pallas_call(
        kernel,
        in_specs=[pl.BlockSpec(memory_space=pltpu.SMEM)]
        + [pl.BlockSpec(memory_space=pltpu.VMEM)] * (len(operands) - 1),
        out_specs=[pl.BlockSpec(memory_space=pltpu.VMEM)] * len(outs),
        out_shape=outs,
        scratch_shapes=scratch,
        compiler_params=pltpu.CompilerParams(vmem_limit_bytes=20 * MIB),
        cost_estimate=pl.CostEstimate(flops=flops, bytes_accessed=0, transcendentals=0),
        name=name,
    )(*operands)


def place(dest, pieces, spot):
    row = 0
    for piece in pieces:
        chips, rows, cols = piece[0].shape
        for k in range(chips):
            for side, ref in enumerate(piece):
                if len(piece) == 1:
                    dest[row : row + rows, :] = ref[k]
                else:
                    block = (spot[0] ^ k) * 2 + (spot[1] ^ side)
                    dest[row : row + rows, pl.ds(pl.multiple_of(block * cols, 128), cols)] = ref[k]
        row += rows


def split_refs(refs, sizes):
    pieces = []
    for size in sizes:
        pieces.append(refs[:size])
        refs = refs[size:]
    return pieces, refs


def dact_kernel(sizes, spot, *refs):
    pieces, (down, dact, dvel) = split_refs(refs, sizes)
    place(dvel, pieces, spot)
    for cols in column_tiles(down.shape[1]):
        dact[:, cols] = jnp.dot(dvel[...], down[:, cols], preferred_element_type=F32)


def dact_of(spot, pieces, down):
    width, hidden = down.shape
    rows = sum(piece[0].shape[1] for piece in pieces)
    return call(
        functools.partial(dact_kernel, [len(piece) for piece in pieces]),
        "dact",
        [spot, *[array for piece in pieces for array in piece], down],
        [jax.ShapeDtypeStruct((rows, hidden), F32)],
        [pltpu.VMEM((rows, width), BF16)],
        2 * rows * width * hidden,
    )[0]


def forward_tiles(h, dact, up, act, dpre):
    for cols in column_tiles(up.shape[1]):
        value, slope = gelu_and_slope(jnp.dot(h[...], up[:, cols], preferred_element_type=F32))
        act[:, cols] = value.astype(BF16)
        dpre[:, cols] = (dact[:, cols] * slope).astype(BF16)


def far_kernel(sizes, spot, *refs):
    pieces, (dact, up, act, dpre, h) = split_refs(refs, sizes)
    place(h, pieces, spot)
    forward_tiles(h, dact, up, act, dpre)


def far_chunk(spot, pieces, dact, up):
    width, hidden = up.shape
    rows = dact.shape[0]
    return call(
        functools.partial(far_kernel, [len(piece) for piece in pieces]),
        "far_tokens",
        [spot, *[array for piece in pieces for array in piece], dact, up],
        [jax.ShapeDtypeStruct((rows, hidden), BF16)] * 2,
        [pltpu.VMEM((rows, width), BF16)],
        2 * rows * width * hidden,
    )


def own_kernel(size, spot, *refs):
    piece, (dact, up, down, act, dpre, *parts, h, block) = split_refs(refs, [size])
    place(h, piece, spot)
    forward_tiles(h, dact, up, act, dpre)
    over = (((1,), (1,)), ((), ()))
    _, chips, _, cols = parts[0].shape
    wide = cols * len(parts)
    for q, (left, weight) in enumerate(((dpre, up), (act, down))):
        for k in range(chips):
            first = 0 if chips == 1 else pl.multiple_of((spot[0] ^ k) * wide, 128)
            block[...] = lax.dot_general(
                left[...], weight[pl.ds(first, wide), :], over, preferred_element_type=F32
            ).astype(BF16)
            for side, part in enumerate(parts):
                if len(parts) == 1:
                    part[q, k] = block[...]
                else:
                    part[q, k] = block[:, pl.ds(pl.multiple_of((spot[1] ^ side) * cols, 128), cols)]


def own_chunk(spot, piece, dact, up, down):
    width, hidden = up.shape
    chips, rows, cols = piece[0].shape
    return call(
        functools.partial(own_kernel, len(piece)),
        "own_tokens",
        [spot, *piece, dact, up, down],
        [jax.ShapeDtypeStruct((rows, hidden), BF16)] * 2
        + [jax.ShapeDtypeStruct((2, chips, rows, cols), BF16)] * len(piece),
        [pltpu.VMEM((rows, width), BF16), pltpu.VMEM((rows, cols * len(piece)), BF16)],
        6 * rows * width * hidden,
    )


def grad_kernel(sizes, groups, spot, *refs):
    both, refs = split_refs(refs, sizes * 2)
    acts, dpres = refs[:groups], refs[groups : 2 * groups]
    grad_up, grad_down, left, out, sems = refs[2 * groups :]
    over = (((0,), (0,)), ((), ()))
    copies = [None, None]
    turn = 0
    for grad, pieces, rights in ((grad_down, both[len(sizes) :], acts), (grad_up, both[: len(sizes)], dpres)):
        row = 0
        for piece in pieces:
            _, rows, cols = piece[0].shape
            for side, ref in enumerate(piece):
                if len(piece) == 1:
                    left[row : row + rows, :] = ref[0]
                else:
                    start = pl.multiple_of((spot[1] ^ side) * cols, 128)
                    left[row : row + rows, pl.ds(start, cols)] = ref[spot[2]]
            row += rows
        for cols in column_tiles(grad.shape[1]):
            row, total = 0, None
            for right in rights:
                rows = right.shape[0]
                part = lax.dot_general(left[row : row + rows], right[:, cols], over, preferred_element_type=F32)
                total = part if total is None else total + part
                row += rows
            slot = turn % 2
            if copies[slot] is not None:
                copies[slot].wait()
            out[slot] = total
            copies[slot] = pltpu.make_async_copy(out.at[slot], grad.at[:, cols], sems.at[slot])
            copies[slot].start()
            turn += 1
    for copy in copies:
        if copy is not None:
            copy.wait()


def weight_grads(spot, h_pieces, d_pieces, acts, dpres, height):
    hidden = acts[0].shape[1]
    tokens = sum(act.shape[0] for act in acts)
    tile = column_tiles(hidden)[0].stop
    operands = [spot, *[array for piece in h_pieces + d_pieces for array in piece], *acts, *dpres]
    return pl.pallas_call(
        functools.partial(grad_kernel, [len(piece) for piece in h_pieces], len(acts)),
        in_specs=[pl.BlockSpec(memory_space=pltpu.SMEM)]
        + [pl.BlockSpec(memory_space=pltpu.VMEM)] * (len(operands) - 1),
        out_specs=[pl.BlockSpec(memory_space=pl.ANY)] * 2,
        out_shape=[jax.ShapeDtypeStruct((height, hidden), F32)] * 2,
        scratch_shapes=[
            pltpu.VMEM((tokens, height), BF16),
            pltpu.VMEM((2, height, tile), F32),
            pltpu.SemaphoreType.DMA((2,)),
        ],
        compiler_params=pltpu.CompilerParams(vmem_limit_bytes=20 * MIB),
        cost_estimate=pl.CostEstimate(
            flops=4 * tokens * height * hidden, bytes_accessed=8 * height * hidden, transcendentals=0
        ),
        name="weight_grads",
    )(*operands)


def swap(value, axis, bits):
    size = lax.axis_size(axis)
    return lax.ppermute(value, axis, [(i, i ^ bits) for i in range(size)])


def chip_sum(value, chips):
    value = value + swap(value, "tensor", 1)
    parts = [swap(value, "tensor", 2 * k) for k in range(1, chips)]
    return sum(parts, value)


def spread(value, chips):
    return jnp.stack([value] + [swap(value, "tensor", 2 * k) for k in range(1, chips)])


def on_device(tokens, buckets, modulation, up_weight, down_weight, output_cotangent):
    rows, cols = tokens.shape
    chips = lax.axis_size("tensor") // 2
    groups = lax.axis_size("dp")
    width = cols * chips * 2
    blocked = cols % 128 == 0 and chips == groups
    place_in_tensor, group = lax.axis_index("tensor"), lax.axis_index("dp")
    chip, core = place_in_tensor // 2, place_in_tensor % 2
    spot = jnp.stack([chip, core, chip ^ group]).astype(jnp.int32)
    order = chip ^ jnp.arange(chips)

    def with_sibling(blocks):
        other = swap(blocks, "tensor", 1)
        if blocked:
            return blocks, other
        pair = jnp.stack([jnp.where(core == 0, blocks, other), jnp.where(core == 0, other, blocks)], axis=1)
        return (jnp.take(pair, order, axis=0).transpose(2, 0, 1, 3).reshape(1, blocks.shape[1], width),)

    x = tokens.astype(F32)
    cot = output_cotangent.astype(F32)
    cond = modulation.at[buckets].get(mode="promise_in_bounds")
    shift, scale, gate = cond[:, 0], cond[:, 1], cond[:, 2]
    dvel = (cot * gate).astype(BF16)
    sums = chip_sum(jnp.stack([jnp.sum(x, axis=1), jnp.sum(x * x, axis=1)]), chips)
    mean = sums[0] / width
    rstd = lax.rsqrt(sums[1] / width - mean * mean + 1e-06)[:, None]
    xhat = (x - mean[:, None]) * rstd
    h = (xhat * (1.0 + scale) + shift).astype(BF16)

    def gather(value):
        blocks = spread(value, chips)
        if groups != 4:
            return [[with_sibling(blocks)]] + [[with_sibling(swap(blocks, "dp", m))] for m in range(1, groups)]
        half = rows // 2
        left, right = swap(blocks, "dp", 1), swap(blocks, "dp", 2)
        corner = swap(left[:, :half], "dp", 2), swap(right[:, half:], "dp", 1)
        return [
            [with_sibling(blocks)],
            [with_sibling(left), with_sibling(right)],
            [with_sibling(piece) for piece in corner],
        ]

    d_groups, h_groups = gather(dvel), gather(h)
    acts, dpres = [], []
    for number, (h_pieces, d_pieces) in enumerate(zip(h_groups, d_groups)):
        dact = dact_of(spot, d_pieces, down_weight)
        if number == 0:
            act, dpre, *parts = own_chunk(spot, h_pieces[0], dact, up_weight, down_weight)
        else:
            act, dpre = far_chunk(spot, h_pieces, dact, up_weight)
        acts.append(act)
        dpres.append(dpre)

    if blocked:
        keep, give = parts
    else:
        pair = jnp.take(parts[0].reshape(2, rows, chips, 2, cols).transpose(0, 2, 3, 1, 4), order, axis=1)
        keep = jnp.where(core == 0, pair[:, :, 0], pair[:, :, 1])
        give = jnp.where(core == 0, pair[:, :, 1], pair[:, :, 0])
    mine = keep.astype(F32) + swap(give, "tensor", 1).astype(F32)
    sent = mine.astype(BF16)
    dh, velocity = [
        sum([swap(sent[q, k], "tensor", 2 * k).astype(F32) for k in range(1, chips)], mine[q, 0]) for q in (0, 1)
    ]
    mixed = (x + gate * velocity).astype(BF16)
    dxhat = dh * (1.0 + scale)
    sums = chip_sum(jnp.stack([jnp.sum(dxhat, axis=1), jnp.sum(dxhat * xhat, axis=1)]), chips) / width
    token_grad = cot + rstd * (dxhat - sums[0][:, None] - xhat * sums[1][:, None])

    height = width // groups
    h_pieces, d_pieces = [piece for g in h_groups for piece in g], [piece for g in d_groups for piece in g]
    if not blocked:
        mine_of = lambda piece: (lax.dynamic_slice_in_dim(piece[0], group * height, height, axis=2),)
        h_pieces, d_pieces = [mine_of(piece) for piece in h_pieces], [mine_of(piece) for piece in d_pieces]
    grad_up, grad_down = weight_grads(spot, h_pieces, d_pieces, acts, dpres, height)
    return mixed, token_grad.astype(BF16), grad_up, grad_down


def solution(mesh):
    rows, cols = P("dp", "tensor"), P(None, "tensor")
    return jax.shard_map(
        on_device,
        mesh=mesh,
        in_specs=(rows, P("dp"), P(None, None, "tensor"), cols, cols, rows),
        out_specs=(rows,) * 4,
        check_vma=False,
    )
```

time: 538 us -> 176 us (0.33)
  waiting for transfers between devices: 424 us -> 63.5 us
  matrix products: 50.7 us -> 0 us
  Pallas kernels: 0 us -> 46 us
  starting transfers between devices: 0.43 us -> 46 us
  blocking collectives: 33.4 us -> 0 us
  between operations: 14.2 us -> 1.16 us
    reduce_scatter x4 -> x0, waiting for transfers between devices: 381 us -> none  [the longest x1 175 us: on_device(): lax.psum_scatter(lax.dot_general(cols, dpre, (((0,), (0,)), ((), ())), pr...]
    ppermute x0 -> x39, waiting for transfers between devices: none -> 63.5 us  [swap(): return lax.ppermute(value, axis, [(i, i ^ bits) for i in range(size)])]
    dot_general x6 -> x0, matrix products: 50.7 us -> none  [the longest x1 9.59 us: on_device(): lax.dot_general(cols, act, (((0,), (0,)), ((), ())), preferred_element_ty...]
    pallas_call x0 -> x7, Pallas kernels: none -> 46 us  [the longest x6 33.1 us: call(): pl.pallas_call(kernel, in_specs=[pl.BlockSpec(memory_space=pltpu.SMEM)] +...]
    ppermute x0 -> x39, starting transfers between devices: none -> 46 us  [swap(): return lax.ppermute(value, axis, [(i, i ^ bits) for i in range(size)])]
    all_gather x2 -> x0, waiting for transfers between devices: 41.5 us -> none  [the longest x1 22.8 us: on_device(): full_dvel = lax.all_gather(dvel, 'tensor', axis=1, tiled=True)]
    psum x2 -> x0, blocking collectives: 33.4 us -> none  [the longest x1 18.1 us: on_device(): lax.psum((jnp.sum(input_tokens, axis=1), jnp.sum(input_tokens * input_tok...]
  transfers between devices with their start and end apart: 6 -> 39, of which waited for: 6 -> 10; matrix products, arithmetic and copies ran while one was open for 7% -> 5% of each run, Pallas kernels for 0% -> 26%
where the time goes in v1:
time: 176 us; the launch traced here: 175 us
  waiting for transfers between devices  63.5 us (36%)
  starting transfers between devices  46 us (26%)
  Pallas kernels  46 us (26%)
  local copies, waits for them, and re-layouts  12.5 us (7%)
  other arithmetic  6.17 us (4%)
    ppermute x39, waiting for transfers between devices, swap(): return lax.ppermute(value, axis, [(i, i ^ bits) for i in range(size)])  63.5 us
    ppermute x39, starting transfers between devices, swap(): return lax.ppermute(value, axis, [(i, i ^ bits) for i in range(size)])  46 us
    pallas_call x6, Pallas kernels, call(): pl.pallas_call(kernel, in_specs=[pl.BlockSpec(memory_space=pltpu.SMEM)] +...  33.1 us
    pallas_call x1, Pallas kernels, weight_grads(): pl.pallas_call(functools.partial(grad_kernel, [len(piece) for piece in h_...  12.9 us
    unnamed x40, local copies, waits for them, and re-layouts  8.1 us
    gather x1, local copies, waits for them, and re-layouts, on_device(): cond = modulation.at[buckets].get(mode='promise_in_bounds')  4.09 us
  transfers between devices with their start and end apart: 39, of which 10 were waited for; matrix products, arithmetic and copies ran while one was open for 5% of the time, Pallas kernels for 26%

profile of v1, /device:TPU:0, one launch (start us, length us, event | category | flops | bytes accessed | tf_op | source)
XLA Modules:
  0.0 175.3 jit_solution(14184150386754581833)
XLA Ops:
  3.1 5.0 %collective-permute-start.3 = (f32[2,256]{1,0:T(2,128)S(1)}, f32[2,256]{1,0:T(2,128)S(1)}, u32[]{:S(2)}, u32[]{:S(2)}) collective-permute-start(f32[2,256]{1,0:T(2,128)S(1)} %fusion.23), channel_id=1, source_target_pairs={{0,6},{1,7},{2,4},{3,5},{4,2},{5,3},{6,0},{7,1},{8,14},{9,15},{10,... | collective-permute-start | bytes 6152 | tf_op jit(solution)/shard_map/ppermute | solution.py:210
  8.7 4.1 %gather_fusion = f32[256,3,384]{2,0,1:T(8,128)S(1)} fusion(f32[1000,3,384]{2,0,1:T(8,128)} %param.8, s32[1024]{0:T(1024)S(1)} %pad_clamp_fusion), kind=kCustom, calls=%fused_computation | custom fusion | bytes 2360320 | tf_op jit(solution)/shard_map/gather | solution.py:243
  13.1 3.8 %collective-permute-start.10 = (bf16[256,384]{1,0:T(8,128)(2,1)S(1)}, bf16[256,384]{1,0:T(8,128)(2,1)S(1)}, u32[]{:S(2)}, u32[]{:S(2)}) collective-permute-start(bf16[256,384]{1,0:T(8,128)(2,1)S(1)} %get-tuple-element.38), channel_id=1, source_target_pairs={{0,6},{1,7},{2,4},{3,5},{4,2},{5,3},{6,0},{7,1},{8,14},{9,15},{10,... | collective-permute-start | bytes 589832 | tf_op jit(solution)/shard_map/ppermute | solution.py:210
  17.6 3.7 %collective-permute-start.6 = (bf16[256,384]{1,0:T(8,128)(2,1)S(1)}, bf16[256,384]{1,0:T(8,128)(2,1)S(1)}, u32[]{:S(2)}, u32[]{:S(2)}) collective-permute-start(bf16[256,384]{1,0:T(8,128)(2,1)S(1)} %get-tuple-element.39), channel_id=1, source_target_pairs={{0,6},{1,7},{2,4},{3,5},{4,2},{5,3},{6,0},{7,1},{8,14},{9,15},{10,... | collective-permute-start | bytes 589832 | tf_op jit(solution)/shard_map/ppermute | solution.py:210
  22.9 9.0 %collective-permute-start.4 = (bf16[256,384]{1,0:T(8,128)(2,1)S(1)}, bf16[256,384]{1,0:T(8,128)(2,1)S(1)}, u32[]{:S(2)}, u32[]{:S(2)}) collective-permute-start(bf16[256,384]{1,0:T(8,128)(2,1)S(1)} %get-tuple-element.39), channel_id=1, source_target_pairs={{0,2},{1,3},{2,0},{3,1},{4,6},{5,7},{6,4},{7,5},{8,10},{9,11},{10,... | collective-permute-start | bytes 589832 | tf_op jit(solution)/shard_map/ppermute | solution.py:210
  31.9 10.7 %collective-permute-done.9 = bf16[256,384]{1,0:T(8,128)(2,1)S(1)} collective-permute-done((bf16[256,384]{1,0:T(8,128)(2,1)S(1)}, bf16[256,384]{1,0:T(8,128)(2,1)S(1)}, u32[]{:S(2)}, u32[]{:S(2)}) %collective-permute-start.9) | collective-permute-done | bytes 196640 | tf_op jit(solution)/shard_map/ppermute | solution.py:210
  42.8 7.1 %collective-permute-done.5 = bf16[256,384]{1,0:T(8,128)(2,1)S(1)} collective-permute-done((bf16[256,384]{1,0:T(8,128)(2,1)S(1)}, bf16[256,384]{1,0:T(8,128)(2,1)S(1)}, u32[]{:S(2)}, u32[]{:S(2)}) %collective-permute-start.5) | collective-permute-done | bytes 196640 | tf_op jit(solution)/shard_map/ppermute | solution.py:210
  53.2 3.7 %copy-done = bf16[3072,1536]{1,0:T(8,128)(2,1)S(1)} copy-done((bf16[3072,1536]{1,0:T(8,128)(2,1)S(1)}, bf16[3072,1536]{1,0:T(8,128)(2,1)}, u32[]{:S(2)}) %copy-start) | copy-done | bytes 9437208
  56.9 3.3 %dact.3.refs_2_ = f32[256,1536]{1,0:T(8,128)S(1)} custom-call(s32[3]{0:T(128)S(1)} %pad_add_fusion.spot, bf16[4,256,384]{2,1,0:T(8,128)(2,1)S(1)} %pad_maximum_fusion.1.refs_0_.refs_10_, bf16[4,256,384]{2,1,0:T(8,128)(2,1)S(1)} %collective-permute-done.11.refs_1_.refs_11_, bf16[3072,1536]{1,0:T(8,128)(2,1)S(1)} %copy-done), custom_call_target="tpu_custom_call" | custom-call | flops 2415919104 | tf_op jit(solution)/shard_map/dact/pallas_call | solution.py:32
  60.9 3.7 %copy-done.2 = bf16[3072,1536]{1,0:T(8,128)(2,1)S(1)} copy-done((bf16[3072,1536]{1,0:T(8,128)(2,1)S(1)}, bf16[3072,1536]{1,0:T(8,128)(2,1)}, u32[]{:S(2)}) %copy-start.2) | copy-done | bytes 9437208
  64.6 9.3 %own_tokens.1 = (bf16[256,1536]{1,0:T(8,128)(2,1)S(1)}, bf16[256,1536]{1,0:T(8,128)(2,1)S(1)}, bf16[2,4,256,384]{3,2,1,0:T(8,128)(2,1)S(1)}, bf16[2,4,256,384]{3,2,1,0:T(8,128)(2,1)S(1)}) custom-call(s32[3]{0:T(128)S(1)} %pad_add_fusion.spot, bf16[4,256,384]{2,1,0:T(8,128)(2,1)S(1)} %pad_maximum_fusion.refs_0_, ...), custom_call_target="tpu_custom_call" | custom-call | flops 7247757312 | tf_op jit(solution)/shard_map/own_tokens/pallas_call | solution.py:32
  75.6 18.3 %collective-permute-done.23.refs_0_.refs_2_ = bf16[4,256,384]{2,1,0:T(8,128)(2,1)S(1)} collective-permute-done((bf16[4,256,384]{2,1,0:T(8,128)(2,1)S(1)}, bf16[4,256,384]{2,1,0:T(8,128)(2,1)S(1)}, u32[]{:S(2)}, u32[]{:S(2)}) %collective-permute-start.23) | collective-permute-done | bytes 786464 | tf_op jit(solution)/shard_map/ppermute | solution.py:210
  96.8 5.8 %dact.4.refs_4_ = f32[512,1536]{1,0:T(8,128)S(1)} custom-call(s32[3]{0:T(128)S(1)} %pad_add_fusion.spot, bf16[4,256,384]{2,1,0:T(8,128)(2,1)S(1)} %collective-permute-done.31.refs_0_.refs_12_, bf16[4,256,384]{2,1,0:T(8,128)(2,1)S(1)} %collective-permute-done.32.refs_1_.refs_13_, bf16[4,256,384]{2,1,0:T(8,128)(2,1)S(1)} %collective-permute-done.33.refs_2_.refs_14_, ...), custom_call_target="tpu_custom_call" | custom-call | flops 4831838208 | tf_op jit(solution)/shard_map/dact/pallas_call | solution.py:32
  105.4 7.7 %collective-permute-done.35.refs_0_.refs_16_ = bf16[4,128,384]{2,1,0:T(8,128)(2,1)S(1)} collective-permute-done((bf16[4,128,384]{2,1,0:T(8,128)(2,1)S(1)}, bf16[4,128,384]{2,1,0:T(8,128)(2,1)S(1)}, u32[]{:S(2)}, u32[]{:S(2)}) %collective-permute-start.35) | collective-permute-done | bytes 393248 | tf_op jit(solution)/shard_map/ppermute | solution.py:210
  114.4 2.4 %collective-permute-start.18 = (bf16[256,384]{1,0:T(8,128)(2,1)S(1)}, bf16[256,384]{1,0:T(8,128)(2,1)S(1)}, u32[]{:S(2)}, u32[]{:S(2)}) collective-permute-start(bf16[256,384]{1,0:T(8,128)(2,1)S(1)} %get-tuple-element.33), channel_id=1, source_target_pairs={{0,6},{1,7},{2,4},{3,5},{4,2},{5,3},{6,0},{7,1},{8,14},{9,15},{10,... | collective-permute-start | bytes 589832 | tf_op jit(solution)/shard_map/ppermute | solution.py:210
  116.8 7.4 %far_tokens.2 = (bf16[512,1536]{1,0:T(8,128)(2,1)S(1)}, bf16[512,1536]{1,0:T(8,128)(2,1)S(1)}) custom-call(s32[3]{0:T(128)S(1)} %pad_add_fusion.spot, bf16[4,256,384]{2,1,0:T(8,128)(2,1)S(1)} %collective-permute-done.23.refs_0_.refs_2_, bf16[4,256,384]{2,1,0:T(8,128)(2,1)S(1)} %collective-permute-done.24.refs_1_.refs_3_, ...), custom_call_target="tpu_custom_call" | custom-call | flops 4831838208 | tf_op jit(solution)/shard_map/far_tokens/pallas_call | solution.py:32
  126.3 2.4 %collective-permute-start.15 = (bf16[256,384]{1,0:T(8,128)(2,1)S(1)}, bf16[256,384]{1,0:T(8,128)(2,1)S(1)}, u32[]{:S(2)}, u32[]{:S(2)}) collective-permute-start(bf16[256,384]{1,0:T(8,128)(2,1)S(1)} %get-tuple-element.35), channel_id=1, source_target_pairs={{0,6},{1,7},{2,4},{3,5},{4,2},{5,3},{6,0},{7,1},{8,14},{9,15},{10,... | collective-permute-start | bytes 589832 | tf_op jit(solution)/shard_map/ppermute | solution.py:210
  128.7 2.0 %collective-permute-start.13 = (bf16[256,384]{1,0:T(8,128)(2,1)S(1)}, bf16[256,384]{1,0:T(8,128)(2,1)S(1)}, u32[]{:S(2)}, u32[]{:S(2)}) collective-permute-start(bf16[256,384]{1,0:T(8,128)(2,1)S(1)} %get-tuple-element.37), channel_id=1, source_target_pairs={{0,2},{1,3},{2,0},{3,1},{4,6},{5,7},{6,4},{7,5},{8,10},{9,11},{10,... | collective-permute-start | bytes 589832 | tf_op jit(solution)/shard_map/ppermute | solution.py:210
  130.7 3.3 %dact.5.refs_4_ = f32[256,1536]{1,0:T(8,128)S(1)} custom-call(s32[3]{0:T(128)S(1)} %pad_add_fusion.spot, bf16[4,128,384]{2,1,0:T(8,128)(2,1)S(1)} %collective-permute-done.35.refs_0_.refs_16_, bf16[4,128,384]{2,1,0:T(8,128)(2,1)S(1)} %collective-permute-done.36.refs_1_.refs_17_, bf16[4,128,384]{2,1,0:T(8,128)(2,1)S(1)} %collective-permute-done.37.refs_2_.refs_18_, ...), custom_call_target="tpu_custom_call" | custom-call | flops 2415919104 | tf_op jit(solution)/shard_map/dact/pallas_call | solution.py:32
  135.8 4.5 %collective-permute-done.16 = bf16[256,384]{1,0:T(8,128)(2,1)S(1)} collective-permute-done((bf16[256,384]{1,0:T(8,128)(2,1)S(1)}, bf16[256,384]{1,0:T(8,128)(2,1)S(1)}, u32[]{:S(2)}, u32[]{:S(2)}) %collective-permute-start.16) | collective-permute-done | bytes 196640 | tf_op jit(solution)/shard_map/ppermute | solution.py:210
  140.3 11.4 %collective-permute-done.14 = bf16[256,384]{1,0:T(8,128)(2,1)S(1)} collective-permute-done((bf16[256,384]{1,0:T(8,128)(2,1)S(1)}, bf16[256,384]{1,0:T(8,128)(2,1)S(1)}, u32[]{:S(2)}, u32[]{:S(2)}) %collective-permute-start.14) | collective-permute-done | bytes 196640 | tf_op jit(solution)/shard_map/ppermute | solution.py:210
  152.9 4.1 %far_tokens.3 = (bf16[256,1536]{1,0:T(8,128)(2,1)S(1)}, bf16[256,1536]{1,0:T(8,128)(2,1)S(1)}) custom-call(s32[3]{0:T(128)S(1)} %pad_add_fusion.spot, bf16[4,128,384]{2,1,0:T(8,128)(2,1)S(1)} %collective-permute-done.27.refs_0_.refs_6_, bf16[4,128,384]{2,1,0:T(8,128)(2,1)S(1)} %collective-permute-done.28.refs_1_.refs_7_, ...), custom_call_target="tpu_custom_call" | custom-call | flops 2415919104 | tf_op jit(solution)/shard_map/far_tokens/pallas_call | solution.py:32
  157.0 2.5 %collective-permute-start.22 = (f32[2,256]{1,0:T(2,128)S(1)}, f32[2,256]{1,0:T(2,128)S(1)}, u32[]{:S(2)}, u32[]{:S(2)}) collective-permute-start(f32[2,256]{1,0:T(2,128)S(1)} %fusion.22), channel_id=1, source_target_pairs={{0,6},{1,7},{2,4},{3,5},{4,2},{5,3},{6,0},{7,1},{8,14},{9,15},{10,... | collective-permute-start | bytes 6152 | tf_op jit(solution)/shard_map/ppermute | solution.py:210
  161.4 12.9 %weight_grads.1 = (f32[768,1536]{1,0:T(8,128)}, f32[768,1536]{1,0:T(8,128)}) custom-call(s32[3]{0:T(128)S(1)} %pad_add_fusion.spot, bf16[4,256,384]{2,1,0:T(8,128)(2,1)S(1)} %copy-done.8, bf16[4,256,384]{2,1,0:T(8,128)(2,1)S(1)} %copy-done.10, bf16[4,256,384]{2,1,0:T(8,128)(2,1)S(1)} %collective-permute-done.23.refs_0_.refs_2_, ...), custom_call_target="tpu_custom_call" | custom-call | flops 4831838208 | bytes 9437184 | tf_op jit(solution)/shard_map/weight_grads/pallas_call | solution.py:189
  (127 shorter events, 26.3 us)
Async XLA Ops:
  16.9 25.6 %collective-permute-start.9 = (bf16[256,384]{1,0:T(8,128)(2,1)S(1)}, bf16[256,384]{1,0:T(8,128)(2,1)S(1)}, u32[]{:S(2)}, u32[]{:S(2)}) collective-permute-start(bf16[256,384]{1,0:T(8,128)(2,1)S(1)} %get-tuple-element.38), channel_id=1, source_target_pairs={{0,4},{1,5},{2,6},{3,7},{4,0},{5,1},{6,2},{7,3},{8,12},{9,13},{10,... | collective-permute-start | bytes 589832 | tf_op jit(solution)/shard_map/ppermute | solution.py:210
  17.0 25.6 %collective-permute-start.8 = (bf16[256,384]{1,0:T(8,128)(2,1)S(1)}, bf16[256,384]{1,0:T(8,128)(2,1)S(1)}, u32[]{:S(2)}, u32[]{:S(2)}) collective-permute-start(bf16[256,384]{1,0:T(8,128)(2,1)S(1)} %get-tuple-element.38), channel_id=1, source_target_pairs={{0,2},{1,3},{2,0},{3,1},{4,6},{5,7},{6,4},{7,5},{8,10},{9,11},{10,... | collective-permute-start | bytes 589832 | tf_op jit(solution)/shard_map/ppermute | solution.py:210
  17.6 25.2 %collective-permute-start.6 = (bf16[256,384]{1,0:T(8,128)(2,1)S(1)}, bf16[256,384]{1,0:T(8,128)(2,1)S(1)}, u32[]{:S(2)}, u32[]{:S(2)}) collective-permute-start(bf16[256,384]{1,0:T(8,128)(2,1)S(1)} %get-tuple-element.39), channel_id=1, source_target_pairs={{0,6},{1,7},{2,4},{3,5},{4,2},{5,3},{6,0},{7,1},{8,14},{9,15},{10,... | collective-permute-start | bytes 589832 | tf_op jit(solution)/shard_map/ppermute | solution.py:210
  21.3 28.6 %collective-permute-start.5 = (bf16[256,384]{1,0:T(8,128)(2,1)S(1)}, bf16[256,384]{1,0:T(8,128)(2,1)S(1)}, u32[]{:S(2)}, u32[]{:S(2)}) collective-permute-start(bf16[256,384]{1,0:T(8,128)(2,1)S(1)} %get-tuple-element.39), channel_id=1, source_target_pairs={{0,4},{1,5},{2,6},{3,7},{4,0},{5,1},{6,2},{7,3},{8,12},{9,13},{10,... | collective-permute-start | bytes 589832 | tf_op jit(solution)/shard_map/ppermute | solution.py:210
  22.9 27.0 %collective-permute-start.4 = (bf16[256,384]{1,0:T(8,128)(2,1)S(1)}, bf16[256,384]{1,0:T(8,128)(2,1)S(1)}, u32[]{:S(2)}, u32[]{:S(2)}) collective-permute-start(bf16[256,384]{1,0:T(8,128)(2,1)S(1)} %get-tuple-element.39), channel_id=1, source_target_pairs={{0,2},{1,3},{2,0},{3,1},{4,6},{5,7},{6,4},{7,5},{8,10},{9,11},{10,... | collective-permute-start | bytes 589832 | tf_op jit(solution)/shard_map/ppermute | solution.py:210
  50.2 24.8 %collective-permute-start.31 = (bf16[4,256,384]{2,1,0:T(8,128)(2,1)S(1)}, bf16[4,256,384]{2,1,0:T(8,128)(2,1)S(1)}, u32[]{:S(2)}, u32[]{:S(2)}) collective-permute-start(bf16[4,256,384]{2,1,0:T(8,128)(2,1)S(1)} %pad_maximum_fusion.1.refs_0_.refs_10_), channel_id=1, source_target_pairs={{0,8},{8,0},{16,24},{24,16},{1,9},{9,1},{17,25},{25,17},{2,10},{10... | collective-permute-start | bytes 2359304 | tf_op jit(solution)/shard_map/ppermute | solution.py:210
  51.7 23.3 %collective-permute-start.33 = (bf16[4,256,384]{2,1,0:T(8,128)(2,1)S(1)}, bf16[4,256,384]{2,1,0:T(8,128)(2,1)S(1)}, u32[]{:S(2)}, u32[]{:S(2)}) collective-permute-start(bf16[4,256,384]{2,1,0:T(8,128)(2,1)S(1)} %pad_maximum_fusion.1.refs_0_.refs_10_), channel_id=1, source_target_pairs={{0,16},{8,24},{16,0},{24,8},{1,17},{9,25},{17,1},{25,9},{2,18},{10... | collective-permute-start | bytes 2359304 | tf_op jit(solution)/shard_map/ppermute | solution.py:210
  73.9 28.8 %collective-permute-start.12 = (bf16[2,4,256,384]{3,2,1,0:T(8,128)(2,1)S(1)}, bf16[2,4,256,384]{3,2,1,0:T(8,128)(2,1)}, u32[]{:S(2)}, u32[]{:S(2)}) collective-permute-start(bf16[2,4,256,384]{3,2,1,0:T(8,128)(2,1)S(1)} %get-tuple-element.15), channel_id=1, source_target_pairs={{0,1},{1,0},{2,3},{3,2},{4,5},{5,4},{6,7},{7,6},{8,9},{9,8},{10,11... | collective-permute-start | bytes 4718600 | tf_op jit(solution)/shard_map/ppermute | solution.py:210
  73.9 20.0 %collective-permute-start.23 = (bf16[4,256,384]{2,1,0:T(8,128)(2,1)S(1)}, bf16[4,256,384]{2,1,0:T(8,128)(2,1)S(1)}, u32[]{:S(2)}, u32[]{:S(2)}) collective-permute-start(bf16[4,256,384]{2,1,0:T(8,128)(2,1)S(1)} %pad_maximum_fusion.refs_0_), channel_id=1, source_target_pairs={{0,8},{8,0},{16,24},{24,16},{1,9},{9,1},{17,25},{25,17},{2,10},{10... | collective-permute-start | bytes 2359304 | tf_op jit(solution)/shard_map/ppermute | solution.py:210
  74.5 20.1 %collective-permute-start.25 = (bf16[4,256,384]{2,1,0:T(8,128)(2,1)S(1)}, bf16[4,256,384]{2,1,0:T(8,128)(2,1)S(1)}, u32[]{:S(2)}, u32[]{:S(2)}) collective-permute-start(bf16[4,256,384]{2,1,0:T(8,128)(2,1)S(1)} %pad_maximum_fusion.refs_0_), channel_id=1, source_target_pairs={{0,16},{8,24},{16,0},{24,8},{1,17},{9,25},{17,1},{25,9},{2,18},{10... | collective-permute-start | bytes 2359304 | tf_op jit(solution)/shard_map/ppermute | solution.py:210
  75.0 21.2 %collective-permute-start.32 = (bf16[4,256,384]{2,1,0:T(8,128)(2,1)S(1)}, bf16[4,256,384]{2,1,0:T(8,128)(2,1)S(1)}, u32[]{:S(2)}, u32[]{:S(2)}) collective-permute-start(bf16[4,256,384]{2,1,0:T(8,128)(2,1)S(1)} %collective-permute-done.31.refs_0_.refs_12_), channel_id=1, source_target_pairs={{0,1},{1,0},{2,3},{3,2},{4,5},{5,4},{6,7},{7,6},{8,9},{9,8},{10,11... | collective-permute-start | bytes 2359304 | tf_op jit(solution)/shard_map/ppermute | solution.py:210
  75.1 21.3 %collective-permute-start.34 = (bf16[4,256,384]{2,1,0:T(8,128)(2,1)S(1)}, bf16[4,256,384]{2,1,0:T(8,128)(2,1)S(1)}, u32[]{:S(2)}, u32[]{:S(2)}) collective-permute-start(bf16[4,256,384]{2,1,0:T(8,128)(2,1)S(1)} %collective-permute-done.33.refs_2_.refs_14_), channel_id=1, source_target_pairs={{0,1},{1,0},{2,3},{3,2},{4,5},{5,4},{6,7},{7,6},{8,9},{9,8},{10,11... | collective-permute-start | bytes 2359304 | tf_op jit(solution)/shard_map/ppermute | solution.py:210
  93.9 30.3 %collective-permute-start.27 = (bf16[4,128,384]{2,1,0:T(8,128)(2,1)S(1)}, bf16[4,128,384]{2,1,0:T(8,128)(2,1)S(1)}, u32[]{:S(2)}, u32[]{:S(2)}) collective-permute-start(bf16[4,128,384]{2,1,0:T(8,128)(2,1)S(1)} %slice.93), channel_id=1, source_target_pairs={{0,16},{8,24},{16,0},{24,8},{1,17},{9,25},{17,1},{25,9},{2,18},{10... | collective-permute-start | bytes 1179656 | tf_op jit(solution)/shard_map/ppermute | solution.py:210
  94.6 18.5 %collective-permute-start.35 = (bf16[4,128,384]{2,1,0:T(8,128)(2,1)S(1)}, bf16[4,128,384]{2,1,0:T(8,128)(2,1)S(1)}, u32[]{:S(2)}, u32[]{:S(2)}) collective-permute-start(bf16[4,128,384]{2,1,0:T(8,128)(2,1)S(1)} %slice.95), channel_id=1, source_target_pairs={{0,16},{8,24},{16,0},{24,8},{1,17},{9,25},{17,1},{25,9},{2,18},{10... | collective-permute-start | bytes 1179656 | tf_op jit(solution)/shard_map/ppermute | solution.py:210
  96.3 17.6 %collective-permute-start.24 = (bf16[4,256,384]{2,1,0:T(8,128)(2,1)S(1)}, bf16[4,256,384]{2,1,0:T(8,128)(2,1)S(1)}, u32[]{:S(2)}, u32[]{:S(2)}) collective-permute-start(bf16[4,256,384]{2,1,0:T(8,128)(2,1)S(1)} %collective-permute-done.23.refs_0_.refs_2_), channel_id=1, source_target_pairs={{0,1},{1,0},{2,3},{3,2},{4,5},{5,4},{6,7},{7,6},{8,9},{9,8},{10,11... | collective-permute-start | bytes 2359304 | tf_op jit(solution)/shard_map/ppermute | solution.py:210
  96.3 18.0 %collective-permute-start.26 = (bf16[4,256,384]{2,1,0:T(8,128)(2,1)S(1)}, bf16[4,256,384]{2,1,0:T(8,128)(2,1)S(1)}, u32[]{:S(2)}, u32[]{:S(2)}) collective-permute-start(bf16[4,256,384]{2,1,0:T(8,128)(2,1)S(1)} %collective-permute-done.25.refs_2_.refs_4_), channel_id=1, source_target_pairs={{0,1},{1,0},{2,3},{3,2},{4,5},{5,4},{6,7},{7,6},{8,9},{9,8},{10,11... | collective-permute-start | bytes 2359304 | tf_op jit(solution)/shard_map/ppermute | solution.py:210
  113.9 14.8 %collective-permute-start.38 = (bf16[4,128,384]{2,1,0:T(8,128)(2,1)S(1)}, bf16[4,128,384]{2,1,0:T(8,128)(2,1)S(1)}, u32[]{:S(2)}, u32[]{:S(2)}) collective-permute-start(bf16[4,128,384]{2,1,0:T(8,128)(2,1)S(1)} %collective-permute-done.37.refs_2_.refs_18_), channel_id=1, source_target_pairs={{0,1},{1,0},{2,3},{3,2},{4,5},{5,4},{6,7},{7,6},{8,9},{9,8},{10,11... | collective-permute-start | bytes 1179656 | tf_op jit(solution)/shard_map/ppermute | solution.py:210
  124.3 16.0 %collective-permute-start.16 = (bf16[256,384]{1,0:T(8,128)(2,1)S(1)}, bf16[256,384]{1,0:T(8,128)(2,1)S(1)}, u32[]{:S(2)}, u32[]{:S(2)}) collective-permute-start(bf16[256,384]{1,0:T(8,128)(2,1)S(1)} %get-tuple-element.32), channel_id=1, source_target_pairs={{0,2},{1,3},{2,0},{3,1},{4,6},{5,7},{6,4},{7,5},{8,10},{9,11},{10,... | collective-permute-start | bytes 589832 | tf_op jit(solution)/shard_map/ppermute | solution.py:210
  128.7 23.0 %collective-permute-start.14 = (bf16[256,384]{1,0:T(8,128)(2,1)S(1)}, bf16[256,384]{1,0:T(8,128)(2,1)S(1)}, u32[]{:S(2)}, u32[]{:S(2)}) collective-permute-start(bf16[256,384]{1,0:T(8,128)(2,1)S(1)} %get-tuple-element.36), channel_id=1, source_target_pairs={{0,4},{1,5},{2,6},{3,7},{4,0},{5,1},{6,2},{7,3},{8,12},{9,13},{10,... | collective-permute-start | bytes 589832 | tf_op jit(solution)/shard_map/ppermute | solution.py:210
  128.7 23.0 %collective-permute-start.13 = (bf16[256,384]{1,0:T(8,128)(2,1)S(1)}, bf16[256,384]{1,0:T(8,128)(2,1)S(1)}, u32[]{:S(2)}, u32[]{:S(2)}) collective-permute-start(bf16[256,384]{1,0:T(8,128)(2,1)S(1)} %get-tuple-element.37), channel_id=1, source_target_pairs={{0,2},{1,3},{2,0},{3,1},{4,6},{5,7},{6,4},{7,5},{8,10},{9,11},{10,... | collective-permute-start | bytes 589832 | tf_op jit(solution)/shard_map/ppermute | solution.py:210
  135.8 17.0 %collective-permute-start.28 = (bf16[4,128,384]{2,1,0:T(8,128)(2,1)S(1)}, bf16[4,128,384]{2,1,0:T(8,128)(2,1)S(1)}, u32[]{:S(2)}, u32[]{:S(2)}) collective-permute-start(bf16[4,128,384]{2,1,0:T(8,128)(2,1)S(1)} %collective-permute-done.27.refs_0_.refs_6_), channel_id=1, source_target_pairs={{0,1},{1,0},{2,3},{3,2},{4,5},{5,4},{6,7},{7,6},{8,9},{9,8},{10,11... | collective-permute-start | bytes 1179656 | tf_op jit(solution)/shard_map/ppermute | solution.py:210
  157.0 17.4 %collective-permute-start.22 = (f32[2,256]{1,0:T(2,128)S(1)}, f32[2,256]{1,0:T(2,128)S(1)}, u32[]{:S(2)}, u32[]{:S(2)}) collective-permute-start(f32[2,256]{1,0:T(2,128)S(1)} %fusion.22), channel_id=1, source_target_pairs={{0,6},{1,7},{2,4},{3,5},{4,2},{5,3},{6,0},{7,1},{8,14},{9,15},{10,... | collective-permute-start | bytes 6152 | tf_op jit(solution)/shard_map/ppermute | solution.py:210
  159.4 15.0 %collective-permute-start.21 = (f32[2,256]{1,0:T(2,128)S(1)}, f32[2,256]{1,0:T(2,128)S(1)}, u32[]{:S(2)}, u32[]{:S(2)}) collective-permute-start(f32[2,256]{1,0:T(2,128)S(1)} %fusion.22), channel_id=1, source_target_pairs={{0,4},{1,5},{2,6},{3,7},{4,0},{5,1},{6,2},{7,3},{8,12},{9,13},{10,... | collective-permute-start | bytes 6152 | tf_op jit(solution)/shard_map/ppermute | solution.py:210
  159.4 15.0 %collective-permute-start.20 = (f32[2,256]{1,0:T(2,128)S(1)}, f32[2,256]{1,0:T(2,128)S(1)}, u32[]{:S(2)}, u32[]{:S(2)}) collective-permute-start(f32[2,256]{1,0:T(2,128)S(1)} %fusion.22), channel_id=1, source_target_pairs={{0,2},{1,3},{2,0},{3,1},{4,6},{5,7},{6,4},{7,5},{8,10},{9,11},{10,... | collective-permute-start | bytes 6152 | tf_op jit(solution)/shard_map/ppermute | solution.py:210
  (35 other events, 388.8 us)
